TPU v7x, 32 devices: a whole 2x2x4 slice. The times are simulated.
32 devices in a mesh: rec: 16 (over z, y, x), var: 2 (over core).
Axes of the slice: x: 2, y: 2, z: 4, core: 2. Of those that a mesh axis runs over, the one named last changes fastest.
Arguments:
- records: bfloat16 [32768, 8192], P('rec', 'var'), as said below
- test_matrix: bfloat16 [8192, 256], P('var'), may hold values from -0.0625 to 0.0625
- col_types: int32 [8192], P('var'), may hold values from 0 to 1
- col_groups: int32 [8192], P('var'), may hold values from 0 to 15
- group_weight: float32 [16], replicated, may hold values from 0.5 to 2
Outputs:
- scores_basis: bfloat16 [32768, 256], P(('rec', 'var'))
- projection: bfloat16 [256, 8192], P(None, 'var')
Inputs may be any that keep to these rules, and one draw needn't show every extreme that they name: `records`: every entry is positive.
All inputs are finite; a program needn't handle non-finite values.
Results may differ from a plain program's by a relative error of at most 0.0043.
The roundings to bfloat16 on the way count: a program that leaves them out, or rounds other values in their place, can miss the bound.
Values sent between devices are 32-bit elements; how exact they have to be, the bound alone decides.
A program may use at most 64 MiB of HBM per device.

v0:
```python
import math

import jax
import jax.numpy as jnp
from jax import lax
from jax.sharding import PartitionSpec as P

epsilon = 1e-05
highest = lax.Precision.HIGHEST


def column_factor(col_mean, col_square, col_types, col_weight):
    spread = col_square - col_mean * col_mean
    picked = jnp.where(col_types == 1, lax.rsqrt(col_mean + epsilon), lax.rsqrt(spread + epsilon))
    return picked * col_weight


def row_gram(left, right):
    return lax.dot_general(
        left, right, (((1,), (1,)), ((), ())), precision=highest, preferred_element_type=jnp.float32
    )


def lower_solve(lower, right):
    return lax.linalg.triangular_solve(lower, right, left_side=True, lower=True)


def local(records, test_matrix, col_types, col_groups, group_weight):
    total_rows = records.shape[0] * lax.axis_size("rec")
    values = records.astype(jnp.float32)
    col_sum, col_square = lax.psum((jnp.sum(values, 0), jnp.sum(values * values, 0)), "rec")
    col_mean = col_sum / total_rows
    onehot = (
        col_groups[:, None] == jnp.arange(group_weight.shape[0], dtype=jnp.int32)[None, :]
    ).astype(jnp.float32)
    col_weight = jnp.dot(onehot, group_weight, precision=highest)
    factor = column_factor(col_mean, col_square / total_rows, col_types, col_weight)
    scaled = ((values - col_mean) * factor).astype(jnp.bfloat16)
    partial_sketch = lax.dot_general(
        test_matrix, scaled, (((0,), (1,)), ((), ())), preferred_element_type=jnp.float32
    )
    piece_len = records.shape[0] // lax.axis_size("var")
    sketch = lax.psum(partial_sketch, "var")
    own_rows = lax.dynamic_slice_in_dim(sketch, lax.axis_index("var") * piece_len, piece_len, 1)
    factor_lower = jnp.linalg.cholesky(lax.psum(row_gram(own_rows, own_rows), ("rec", "var")))
    basis_own = lower_solve(factor_lower, own_rows)
    whole_basis = lower_solve(factor_lower, sketch)
    result = jnp.dot(whole_basis, scaled, precision=highest, preferred_element_type=jnp.float32)
    summed = lax.psum(result, "rec")
    summed = summed / math.sqrt(total_rows)
    scores_basis = (basis_own.T * math.sqrt(total_rows)).astype(jnp.bfloat16)
    return (scores_basis, summed.astype(jnp.bfloat16))


def solution(mesh):
    in_specs = (P("rec", "var"), P("var", None), P("var"), P("var"), P())
    out_specs = (P(("rec", "var"), None), P(None, "var"))
    return jax.shard_map(local, mesh=mesh, in_specs=in_specs, out_specs=out_specs, check_vma=False)
```

profile of v0, /device:TPU:0, one launch (start us, length us, event | category | flops | bytes accessed | tf_op | source)
XLA Modules:
  0.0 518.7 jit_solution(11401620359540813519)
XLA Ops:
  7.2 0.0 copy-start
  7.2 0.0 copy-start.3
  7.2 0.0 copy-start.2
  7.2 0.0 copy-start.1
  7.2 0.0 all-reduce.6.cloned.1.call-start
  7.3 7.7 %convert_reduce_fusion = (f32[4096]{0:T(1024)S(1)}, f32[4096]{0:T(1024)S(1)}) fusion(bf16[2048,4096]{1,0:T(8,128)(2,1)} %param.5), kind=kLoop, calls=%fused_computation.4 | loop fusion | flops 33546240 | bytes 16809984 | tf_op jit(solution)/shard_map/reduce_sum | solution.py:31
  15.0 0.0 copy-done.3
  15.0 0.0 copy-done.2
  15.0 0.2 fusion.22
  15.2 78.6 %all-reduce.1 = (f32[4096]{0:T(1024)S(1)}, f32[4096]{0:T(1024)S(1)}) all-reduce(f32[4096]{0:T(1024)S(1)} %get-tuple-element.15, f32[4096]{0:T(1024)S(1)} %get-tuple-element.14), channel_id=1, replica_groups=mesh['rec'=16,'var'=2] {'rec'}, use_global_device_ids=true, to_apply=%region_3.0 | all-reduce | flops 8192 | bytes 65536 | tf_op jit(solution)/shard_map/psum | solution.py:31
  93.8 0.0 copy-done.1
  93.8 0.0 copy-done
  93.8 9.9 %fusion.7 = f32[256,2048]{0,1:T(8,128)} fusion(bf16[4096,256]{1,0:T(8,128)(2,1)S(1)} %copy-done, bf16[2048,4096]{1,0:T(8,128)(2,1)} %param.5, f32[4096]{0:T(1024)S(1)} %get-tuple-element.33, f32[4096]{0:T(1024)S(1)} %get-tuple-element.32), kind=kOutput, calls=%fused_computation.11 | convolution fusion | flops 4328521728 | bytes 21004288 | tf_op jit(solution)/shard_map/dot_general | solution.py:39
  103.7 0.0 all-reduce.6.cloned.1.call-update
  103.7 0.0 all-reduce.8.cloned.1.call-start
  103.8 17.2 %all-reduce.6.cloned.1.call-done = f32[256,2048]{0,1:T(8,128)} async-done(((f32[256,2048]{0,1:T(8,128)}), f32[256,2048]{0,1:T(8,128)}) %all-reduce.6.cloned.1.call-update) | async-done | bytes 2097168 | tf_op jit(solution)/shard_map/psum | solution.py:43
  120.9 4.2 fusion.16
  125.2 0.0 all-reduce.8.cloned.1.call-update
  125.2 0.2 all-reduce.10.cloned.1.call-start
  125.5 128.7 %all-reduce.8.cloned.1.call-done = f32[256,256]{0,1:T(8,128)} async-done(((f32[256,256]{0,1:T(8,128)}), f32[256,256]{0,1:T(8,128)}) %all-reduce.8.cloned.1.call-update) | async-done | bytes 262160 | tf_op jit(solution)/shard_map/psum | solution.py:45
  254.2 1.1 copy.11
  255.3 1.0 fusion.21
  256.3 11.7 %cholesky.50 = f32[128,128]{1,0:T(8,128)S(1)} custom-call(f32[128,128]{1,0:T(8,128)S(1)} %cholesky.118), custom_call_target="Cholesky" | custom-call | tf_op jit(solution)/shard_map/jit(cholesky)/cholesky | solution.py:45
  268.0 9.8 %custom-call.16 = f32[1,128,128]{1,2,0:T(8,128)S(1)} custom-call(f32[1,128,128]{2,1,0:T(8,128)S(1)} %get-tuple-element.31), custom_call_target="InvertDiagBlocksLowerTriangular" | custom-call | tf_op jit(solution)/shard_map/jit(cholesky)/cholesky | solution.py:45
  277.9 0.2 constant_dynamic-update-slice_fusion
  278.1 0.3 convolution_subtract_fusion.2
  278.4 11.7 %cholesky.105 = f32[128,128]{1,0:T(8,128)S(1)} custom-call(f32[128,128]{1,0:T(8,128)S(1)} %convolution_subtract_fusion.2), custom_call_target="Cholesky" | custom-call | tf_op jit(solution)/shard_map/jit(cholesky)/cholesky | solution.py:45
  290.1 0.7 compare_reduce_fusion
  292.2 0.1 triangular_solve.72
  292.3 4.3 while.1
  292.5 0.6 fusion.44
  293.1 1.4 bitcast_dynamic-update-slice_fusion.2
  294.5 0.6 fusion.44
  295.1 1.4 bitcast_dynamic-update-slice_fusion.2
  296.6 19.7 %custom-call.17 = f32[2,128,128]{1,2,0:T(8,128)S(1)} custom-call(f32[2,128,128]{2,1,0:T(8,128)S(1)} %get-tuple-element.9), custom_call_target="InvertDiagBlocksLowerTriangular" | custom-call | tf_op jit(solution)/shard_map/triangular_solve | solution.py:25
  316.3 2.3 fusion.13
  318.6 3.0 convolution_subtract_fusion
  321.6 1.1 fusion.27
  322.7 18.2 %fusion.3 = f32[256,4096]{1,0:T(8,128)} fusion(bf16[2048,4096]{1,0:T(8,128)(2,1)} %param.5, f32[4096]{0:T(1024)S(1)} %get-tuple-element.33, f32[4096]{0:T(1024)S(1)} %get-tuple-element.32, f32[128,2048]{1,0:T(8,128)S(1)} %fusion.27, f32[128,2048]{1,0:T(8,128)S(1)} %fusion.13), kind=kOutput, calls=%fused_computation.8 | convolution fusion | flops 25803882496 | bytes 23101440 | tf_op jit(solution)/shard_map/dot_general | solution.py:48
  340.9 0.0 all-reduce.10.cloned.1.call-update
  340.9 1.7 fusion.19
  342.6 2.0 convolution_subtract_fusion.1
  344.7 0.6 fusion.28
  345.3 0.1 fusion.18
  345.4 1.0 copy.12
  346.4 161.8 %all-reduce.10.cloned.1.call-done = f32[256,4096]{1,0:T(8,128)} async-done(((f32[256,4096]{1,0:T(8,128)}), f32[256,4096]{1,0:T(8,128)}) %all-reduce.10.cloned.1.call-update) | async-done | bytes 4194320 | tf_op jit(solution)/shard_map/psum | solution.py:49
  508.3 3.9 multiply_convert_fusion
  (10 shorter events, 0.2 us)
Async XLA Ops:
  7.2 86.6 %copy-start = (bf16[4096,256]{1,0:T(8,128)(2,1)S(1)}, bf16[4096,256]{1,0:T(8,128)(2,1)}, u32[]{:S(2)}) copy-start(bf16[4096,256]{1,0:T(8,128)(2,1)} %param.6) | copy-start | bytes 6291460
  7.2 7.8 %copy-start.3 = (f32[16]{0:T(128)S(1)}, f32[16]{0:T(128)}, u32[]{:S(2)}) copy-start(f32[16]{0:T(128)} %param.9) | copy-start | bytes 196
  7.2 7.8 %copy-start.2 = (s32[4096]{0:T(1024)S(1)}, s32[4096]{0:T(1024)}, u32[]{:S(2)}) copy-start(s32[4096]{0:T(1024)} %param.8) | copy-start | bytes 49156
  7.2 86.6 %copy-start.1 = (s32[4096]{0:T(1024)S(1)}, s32[4096]{0:T(1024)}, u32[]{:S(2)}) copy-start(s32[4096]{0:T(1024)} %param.7) | copy-start | bytes 49156
  7.2 113.7 %all-reduce.6.cloned.1.call-start = ((), (), s32[]{:S(2)}) async-start(), calls=%async_computation | async-start | bytes 4194304 | tf_op jit(solution)/shard_map/psum | solution.py:43
  103.7 150.5 %all-reduce.8.cloned.1.call-start = ((), (), s32[]{:S(2)}) async-start(), calls=%async_computation.1 | async-start | bytes 524288 | tf_op jit(solution)/shard_map/psum | solution.py:45
  125.2 383.1 %all-reduce.10.cloned.1.call-start = ((), (), s32[]{:S(2)}) async-start(), calls=%async_computation.2 | async-start | bytes 8388608 | tf_op jit(solution)/shard_map/psum | solution.py:49
Sparse Core Ops, SparseCore 0:
  103.8 17.0 all-reduce.5
  127.9 126.2 all-reduce.7
  341.1 167.1 all-reduce.9
where the time goes:
time: 519 us
  waiting for transfers between devices  308 us (59%)
  blocking collectives  78.6 us (15%)
  other arithmetic  66.4 us (13%)
  matrix products  43.8 us (8%)
  between operations  15.3 us (3%)
  local copies, waits for them, and re-layouts  6.25 us (1%)
    psum x1, waiting for transfers between devices, local(): summed = lax.psum(result, 'rec')  162 us
    psum x1, waiting for transfers between devices, local(): lax.psum(row_gram(own_rows, own_rows), ('rec', 'var'))  129 us
    psum x1, blocking collectives, local(): lax.psum((jnp.sum(values, 0), jnp.sum(values * values, 0)), 'rec')  78.6 us
    another operation x6, other arithmetic, local(): jnp.linalg.cholesky(lax.psum(row_gram(own_rows, own_rows), ('rec', 'var')))  34 us
    another operation x3, other arithmetic, lower_solve(): return lax.linalg.triangular_solve(lower, right, left_side=True, lower=True)  19.7 us
    dot_general x1, matrix products, local(): jnp.dot(whole_basis, scaled, precision=highest, preferred_element_type=jn...  18.2 us
    psum x1, waiting for transfers between devices, local(): sketch = lax.psum(partial_sketch, 'var')  17.2 us
    another operation x6, matrix products, lower_solve(): return lax.linalg.triangular_solve(lower, right, left_side=True, lower=True)  10.8 us
  transfers between devices with their start and end apart: 3, of which 3 were waited for; matrix products, arithmetic and copies ran while one was open for 1% of the time, Pallas kernels for 0%

commit v1 on v0

v1 whole, which is shorter than its diff:
```python
import functools
import math

import jax
import jax.numpy as jnp
from jax import lax
from jax.experimental import pallas as pl
from jax.experimental.pallas import tpu as pltpu
from jax.sharding import PartitionSpec as P

epsilon = 1e-05
highest = lax.Precision.HIGHEST
MESH = pl.DeviceIdType.MESH
LANES = 128
BLOCK = 64
QUARTERS = 4


def column_factor(col_mean, col_square, col_types, col_weight):
    spread = col_square - col_mean * col_mean
    picked = jnp.where(col_types == 1, lax.rsqrt(col_mean + epsilon), lax.rsqrt(spread + epsilon))
    return picked * col_weight


def rec_groups(n_rec):
    groups, shift = [], 1
    while shift < n_rec:
        size = min(4, n_rec // shift)
        groups.append((shift, size))
        shift *= size
    return groups


def group_place(me, shift, size):
    return lax.rem(lax.div(me, shift), size)


def greet(me, groups, my_var, n_var):
    barrier = pltpu.get_barrier_semaphore()
    count = 0
    for shift, size in groups:
        place = group_place(me, shift, size)
        for k in range(1, size):
            other = me + (lax.rem(place + k, size) - place) * shift
            pl.semaphore_signal(barrier, inc=1, device_id=(other, my_var), device_id_type=MESH)
            count += 1
    for k in range(1, n_var):
        pl.semaphore_signal(barrier, inc=1, device_id=(me, lax.rem(my_var + k, n_var)), device_id_type=MESH)
        count += 1
    pl.semaphore_wait(barrier, count)


def group_sum(value, buf, send_sem, recv_sem, me, my_var, shift, size):
    place = group_place(me, shift, size)
    buf[place] = value
    copies = []
    for k in range(1, size):
        other = me + (lax.rem(place + k, size) - place) * shift
        copy = pltpu.make_async_remote_copy(
            src_ref=buf.at[place], dst_ref=buf.at[place], send_sem=send_sem.at[k], recv_sem=recv_sem.at[k],
            device_id=(other, my_var), device_id_type=MESH)
        copy.start()
        copies.append(copy)
    for copy in copies:
        copy.wait()
    total = buf[0]
    for i in range(1, size):
        total = total + buf[i]
    return total


def stats_kernel(n_rec, x_ref, o_ref, buf, send_sem, recv_sem):
    me, my_var = lax.axis_index("rec"), lax.axis_index("var")
    groups = rec_groups(n_rec)
    greet(me, groups, my_var, 1)
    current = x_ref[...]
    for g, (shift, size) in enumerate(groups):
        current = group_sum(current, buf.at[g], send_sem.at[g], recv_sem.at[g], me, my_var, shift, size)
    o_ref[...] = current


def sum_over_rec(x, n_rec):
    n_groups = len(rec_groups(n_rec))
    return pl.pallas_call(
        functools.partial(stats_kernel, n_rec),
        out_shape=jax.ShapeDtypeStruct(x.shape, x.dtype),
        in_specs=[pl.BlockSpec(memory_space=pltpu.VMEM)],
        out_specs=pl.BlockSpec(memory_space=pltpu.VMEM),
        scratch_shapes=[
            pltpu.VMEM((n_groups, 4) + x.shape, jnp.float32),
            pltpu.SemaphoreType.DMA((n_groups, 4)),
            pltpu.SemaphoreType.DMA((n_groups, 4)),
        ],
        compiler_params=pltpu.CompilerParams(collective_id=0, has_side_effects=True, vmem_limit_bytes=16 << 20),
    )(x)


def rows_at(start, size):
    return pl.ds(pl.multiple_of(start, 8), size)


def lanes_at(start, size):
    return pl.ds(pl.multiple_of(start, LANES), size)


def factor_block(block):
    tiles_n = BLOCK // 8
    lane = lax.broadcasted_iota(jnp.int32, (8, LANES), 1)
    row = lax.broadcasted_iota(jnp.int32, (8, LANES), 0)
    tiles = []
    for t in range(tiles_n):
        eye = (lane == row + (BLOCK + 8 * t)).astype(jnp.float32)
        tiles.append(jnp.where(lane < BLOCK, block[8 * t:8 * t + 8, :], eye))
    for j in range(BLOCK - 1):
        own, sub = j // 8, j % 8
        pivot_row = tiles[own][sub:sub + 1, :]
        scaled_row = pivot_row / pivot_row[:, j:j + 1]
        if sub < 7:
            below = jnp.where(row > sub, jnp.broadcast_to(tiles[own][:, j:j + 1], (8, LANES)), 0.0)
            tiles[own] = tiles[own] - below * scaled_row
        for t in range(own + 1, tiles_n):
            tiles[t] = tiles[t] - tiles[t][:, j:j + 1] * scaled_row
    done = []
    for t in range(tiles_n):
        pivots = jnp.sum(jnp.where(lane == row + 8 * t, tiles[t], 0.0), axis=1, keepdims=True)
        done.append(tiles[t] / jnp.sqrt(pivots))
    whole = jnp.concatenate(done, axis=0)
    return pltpu.roll(whole, BLOCK, axis=1)[:, :BLOCK]


def stage_plan(n_rec, columns):
    bits = n_rec.bit_length() - 1
    high = list(range(bits - 1, 1, -1))
    orders = [[0, 1] + high, [1, 0] + high]
    halvings = min(bits, (columns // (2 * LANES)).bit_length() - 1)
    return orders, halvings


def main_kernel(n_rec, n_var, total_rows, s_ref, y_ref, scores_ref, out_ref,
                y_buf, got, full, gram, gram_rs, gram_ar, aug,
                rs_send, rs_recv, ag_send, ag_recv, g_send, g_recv, y_sem):
    me, my_var = lax.axis_index("rec"), lax.axis_index("var")
    k_dim, columns = y_buf.shape
    groups = rec_groups(n_rec)
    orders, halvings = stage_plan(n_rec, columns)
    n_stages = len(orders[0])
    part_cols = columns // 2
    part_rows = k_dim // QUARTERS
    load = pltpu.make_async_copy(y_ref, y_buf, y_sem)
    load.start()

    greet(me, groups, my_var, n_var)

    def bit_of(j):
        return lax.rem(lax.div(me, 1 << j), 2)

    def peer_of(j):
        return me + (1 - 2 * bit_of(j)) * (1 << j)

    bases = []
    for p in range(2):
        base, held, width = [jnp.int32(p * part_cols)], [part_cols], part_cols
        for s in range(halvings):
            width //= 2
            base.append(base[-1] + bit_of(orders[p][s]) * width)
            held.append(width)
        for s in range(halvings, n_stages):
            base.append(base[-1])
            held.append(width)
        bases.append((base, held))
    got_at, at = [], 0
    for s in range(n_stages):
        got_at.append(at)
        at += bases[0][1][s + 1]

    def rs_copy(p, q, s):
        base, held = bases[p]
        width = held[s + 1]
        if s < halvings:
            start = base[s] + (1 - bit_of(orders[p][s])) * width
        else:
            start = base[s]
        rows = pl.ds(q * part_rows, part_rows)
        return pltpu.make_async_remote_copy(
            src_ref=y_buf.at[rows, lanes_at(start, width)],
            dst_ref=got.at[p, rows, pl.ds(got_at[s], width)],
            send_sem=rs_send.at[p, q, s], recv_sem=rs_recv.at[p, q, s],
            device_id=(peer_of(orders[p][s]), my_var), device_id_type=MESH)

    def rs_step(t):
        for q in range(QUARTERS):
            s = t - q
            if s < 0 or s > n_stages:
                continue
            for p in range(2):
                if s > 0:
                    rs_copy(p, q, s - 1).wait()
                    base, held = bases[p]
                    rows = pl.ds(q * part_rows, part_rows)
                    lanes = lanes_at(base[s], held[s])
                    y_buf[rows, lanes] = y_buf[rows, lanes] + got[p, rows, pl.ds(got_at[s - 1], held[s])]
                if s < n_stages:
                    rs_copy(p, q, s).start()

    rs_left = list(range(QUARTERS + n_stages))

    def advance(n=1):
        for _ in range(n):
            if rs_left:
                rs_step(rs_left.pop(0))

    rows_dev = s_ref.shape[0]
    step_rows = 256

    def gram_step(i, total):
        part = s_ref[rows_at(i * step_rows, step_rows), :]
        return total + lax.dot_general(part, part, (((0,), (0,)), ((), ())), precision=highest,
                                       preferred_element_type=jnp.float32)

    gram[0] = lax.fori_loop(0, rows_dev // step_rows, gram_step, jnp.zeros((k_dim, k_dim), jnp.float32))
    half = k_dim // n_var
    shift, size = groups[0]
    piece = half // size
    place = group_place(me, shift, size)
    copies = []
    for k in range(1, size):
        other_place = lax.rem(place + k, size)
        copy = pltpu.make_async_remote_copy(
            src_ref=gram.at[0, rows_at(my_var * half + other_place * piece, piece), :],
            dst_ref=gram_rs.at[place],
            send_sem=g_send.at[0, k], recv_sem=g_recv.at[0, k],
            device_id=(me + (other_place - place) * shift, my_var), device_id_type=MESH)
        copy.start()
        copies.append(copy)
    own_rows = rows_at(my_var * half + place * piece, piece)
    gram_rs[place] = gram[0, own_rows, :]
    load.wait()
    for copy in copies:
        copy.wait()
    current = gram_rs[0]
    for i in range(1, size):
        current = current + gram_rs[i]
    for g in range(1, len(groups)):
        current = group_sum(current, gram_ar.at[g - 1], g_send.at[g], g_recv.at[g], me, my_var, *groups[g])
    gram[1, own_rows, :] = current
    copies = []
    last = len(groups)
    for k in range(1, size):
        other_place = lax.rem(place + k, size)
        copy = pltpu.make_async_remote_copy(
            src_ref=gram.at[1, own_rows, :], dst_ref=gram.at[1, own_rows, :],
            send_sem=g_send.at[last, k], recv_sem=g_recv.at[last, k],
            device_id=(me + (other_place - place) * shift, my_var), device_id_type=MESH)
        copy.start()
        copies.append(copy)
    for copy in copies:
        copy.wait()
    copies = []
    half_rows = rows_at(my_var * half, half)
    for k in range(1, n_var):
        copy = pltpu.make_async_remote_copy(
            src_ref=gram.at[1, half_rows, :], dst_ref=gram.at[1, half_rows, :],
            send_sem=g_send.at[last + 1, k], recv_sem=g_recv.at[last + 1, k],
            device_id=(me, lax.rem(my_var + k, n_var)), device_id_type=MESH)
        copy.start()
        copies.append(copy)
    advance()
    for copy in copies:
        copy.wait()

    aug[:, :k_dim] = gram[1]
    wide_row = lax.broadcasted_iota(jnp.int32, (k_dim, k_dim), 0)
    wide_lane = lax.broadcasted_iota(jnp.int32, (k_dim, k_dim), 1)
    aug[:, k_dim:] = (wide_row == wide_lane).astype(jnp.float32)
    n_blocks = k_dim // BLOCK
    for b in range(n_blocks):
        rows = slice(b * BLOCK, (b + 1) * BLOCK)
        lane_at = b * BLOCK // LANES * LANES
        block = aug[rows, lane_at:lane_at + LANES]
        if b * BLOCK != lane_at:
            block = pltpu.roll(block, LANES - BLOCK, axis=1)
        inverse = factor_block(block)
        advance()
        solved = jnp.dot(inverse, aug[rows, :], precision=highest, preferred_element_type=jnp.float32)
        aug[rows, :] = solved
        if b + 1 < n_blocks:
            change = lax.dot_general(solved[:, :k_dim], solved, (((0,), (0,)), ((), ())), precision=highest,
                                     preferred_element_type=jnp.float32)
            rest = slice((b + 1) * BLOCK, k_dim)
            aug[rest, :] = aug[rest, :] - change[rest, :]
            advance()
    advance(len(rs_left))

    for p in range(2):
        base, held = bases[p]
        lanes = lanes_at(base[-1], held[-1])
        full[:, lanes] = jnp.dot(aug[:, k_dim:], y_buf[:, lanes], precision=highest,
                                 preferred_element_type=jnp.float32) * (1.0 / math.sqrt(total_rows))

    def ag_copy(p, q, s):
        base, held = bases[p]
        place_now = (pl.ds(q * part_rows, part_rows), lanes_at(base[s + 1], held[s + 1]))
        return pltpu.make_async_remote_copy(
            src_ref=full.at[place_now], dst_ref=full.at[place_now],
            send_sem=ag_send.at[p, q, s], recv_sem=ag_recv.at[p, q, s],
            device_id=(peer_of(orders[p][s]), my_var), device_id_type=MESH)

    own = rows_dev // n_var
    for t in range(QUARTERS + halvings):
        for q in range(QUARTERS):
            s = halvings - 1 - (t - q)
            if s < -1 or s > halvings - 1:
                continue
            for p in range(2):
                if s < halvings - 1:
                    ag_copy(p, q, s + 1).wait()
                if s >= 0:
                    ag_copy(p, q, s).start()
            if s == -1:
                rows = slice(q * part_rows, (q + 1) * part_rows)
                out_ref[rows, :] = full[rows, :].astype(out_ref.dtype)
        if t < 4:
            n = own // 4
            mine = s_ref[rows_at(my_var * own + t * n, n), :]
            basis = lax.dot_general(mine, aug[:, k_dim:], (((1,), (1,)), ((), ())), precision=highest,
                                    preferred_element_type=jnp.float32)
            scores_ref[t * n:(t + 1) * n, :] = (basis * math.sqrt(total_rows)).astype(scores_ref.dtype)


def factor_and_project(sketch, products, n_rec, n_var, total_rows):
    rows_dev, k_dim = sketch.shape
    columns = products.shape[1]
    groups = rec_groups(n_rec)
    orders, halvings = stage_plan(n_rec, columns)
    n_stages = len(orders[0])
    width, got_width = columns // 2, 0
    for s in range(n_stages):
        if s < halvings:
            width //= 2
        got_width += width
    piece = k_dim // n_var // groups[0][1]
    vmem = pl.BlockSpec(memory_space=pltpu.VMEM)
    dma = pltpu.SemaphoreType.DMA
    return pl.pallas_call(
        functools.partial(main_kernel, n_rec, n_var, total_rows),
        out_shape=(
            jax.ShapeDtypeStruct((rows_dev // n_var, k_dim), jnp.bfloat16),
            jax.ShapeDtypeStruct((k_dim, columns), jnp.bfloat16),
        ),
        in_specs=[vmem, pl.BlockSpec(memory_space=pl.ANY)],
        out_specs=(vmem, vmem),
        scratch_shapes=[
            pltpu.VMEM((k_dim, columns), jnp.float32),
            pltpu.VMEM((2, k_dim, got_width), jnp.float32),
            pltpu.VMEM((k_dim, columns), jnp.float32),
            pltpu.VMEM((2, k_dim, k_dim), jnp.float32),
            pltpu.VMEM((groups[0][1], piece, k_dim), jnp.float32),
            pltpu.VMEM((max(1, len(groups) - 1), 4, piece, k_dim), jnp.float32),
            pltpu.VMEM((k_dim, 2 * k_dim), jnp.float32),
            dma((2, QUARTERS, n_stages)), dma((2, QUARTERS, n_stages)),
            dma((2, QUARTERS, n_stages)), dma((2, QUARTERS, n_stages)),
            dma((len(groups) + 2, max(4, n_var))), dma((len(groups) + 2, max(4, n_var))),
            dma,
        ],
        compiler_params=pltpu.CompilerParams(collective_id=1, has_side_effects=True, vmem_limit_bytes=48 << 20),
    )(sketch, products)


def local(records, test_matrix, col_types, col_groups, group_weight):
    n_rec, n_var = lax.axis_size("rec"), lax.axis_size("var")
    total_rows = records.shape[0] * n_rec
    columns = records.shape[1]
    values = records.astype(jnp.float32)
    sums = jnp.concatenate([jnp.sum(values, 0), jnp.sum(values * values, 0)]).reshape(-1, LANES)
    sums = sum_over_rec(sums, n_rec).reshape(2, columns)
    col_mean = sums[0] / total_rows
    onehot = (
        col_groups[:, None] == jnp.arange(group_weight.shape[0], dtype=jnp.int32)[None, :]
    ).astype(jnp.float32)
    col_weight = jnp.dot(onehot, group_weight, precision=highest)
    factor = column_factor(col_mean, sums[1] / total_rows, col_types, col_weight)
    scaled = ((values - col_mean) * factor).astype(jnp.bfloat16)
    partial_sketch = jnp.dot(scaled, test_matrix, preferred_element_type=jnp.float32)
    sketch = lax.psum(partial_sketch, "var")
    upper = sketch.astype(jnp.bfloat16)
    lower = (sketch - upper.astype(jnp.float32)).astype(jnp.bfloat16)
    both = jnp.concatenate([upper, lower], axis=1)
    pair = lax.dot_general(both, scaled, (((0,), (0,)), ((), ())), preferred_element_type=jnp.float32)
    k_dim = test_matrix.shape[1]
    products = pair[:k_dim] + pair[k_dim:]
    return factor_and_project(sketch, products, n_rec, n_var, total_rows)


def solution(mesh):
    in_specs = (P("rec", "var"), P("var", None), P("var"), P("var"), P())
    out_specs = (P(("rec", "var"), None), P(None, "var"))
    return jax.shard_map(local, mesh=mesh, in_specs=in_specs, out_specs=out_specs, check_vma=False)
```

time: 519 us -> 219 us (0.42)
  waiting for transfers between devices: 308 us -> 20.8 us
  Pallas kernels: 0 us -> 147 us
  blocking collectives: 78.6 us -> 0 us
  other arithmetic: 66.4 us -> 12.9 us
  matrix products: 43.8 us -> 22.1 us
    psum x2 -> x0, waiting for transfers between devices: 291 us -> none  [the longest x1 162 us: local(): summed = lax.psum(result, 'rec')]
    pallas_call x0 -> x2, Pallas kernels: none -> 147 us  [the longest x1 134 us: factor_and_project(): pl.pallas_call(functools.partial(main_kernel, n_rec, n_var, total_rows),...]
    psum x1 -> x0, blocking collectives: 78.6 us -> none  [local(): lax.psum((jnp.sum(values, 0), jnp.sum(values * values, 0)), 'rec')]
    another operation x9 -> x0, other arithmetic: 53.7 us -> none  [the longest x6 34 us: local(): jnp.linalg.cholesky(lax.psum(row_gram(own_rows, own_rows), ('rec', 'var')))]
    another operation x8 -> x0, matrix products: 11.2 us -> none  [the longest x6 10.8 us: lower_solve(): return lax.linalg.triangular_solve(lower, right, left_side=True, lower=True)]
    dot_general x3 -> x2, matrix products: 32.4 us -> 21.9 us  [the longest x1 12 us: local(): lax.dot_general(both, scaled, (((0,), (0,)), ((), ())), preferred_element...]
  transfers between devices with their start and end apart: 3 -> 1, of which waited for: 3 -> 1; matrix products, arithmetic and copies ran while one was open for 1% -> 0% of each run, Pallas kernels for 0% -> 0%
where the time goes in v1:
time: 219 us
  Pallas kernels  147 us (67%)
  matrix products  22.1 us (10%)
  waiting for transfers between devices  20.8 us (9%)
  between operations  14.2 us (6%)
  other arithmetic  12.9 us (6%)
    pallas_call x1, Pallas kernels, factor_and_project(): pl.pallas_call(functools.partial(main_kernel, n_rec, n_var, total_rows),...  134 us
    psum x1, waiting for transfers between devices, local(): sketch = lax.psum(partial_sketch, 'var')  20.7 us
    pallas_call x1, Pallas kernels, sum_over_rec(): pl.pallas_call(functools.partial(stats_kernel, n_rec), out_shape=jax.Shap...  12.8 us
    dot_general x1, matrix products, local(): lax.dot_general(both, scaled, (((0,), (0,)), ((), ())), preferred_element...  12 us
    dot_general x1, matrix products, local(): jnp.dot(scaled, test_matrix, preferred_element_type=jnp.float32)  9.88 us
    reduce_sum x1, other arithmetic, local(): jnp.sum(values, 0)  7.72 us
  transfers between devices with their start and end apart: 1, of which 1 were waited for; matrix products, arithmetic and copies ran while one was open for 0% of the time, Pallas kernels for 0%

profile of v1, /device:TPU:0, one launch (start us, length us, event | category | flops | bytes accessed | tf_op | source)
XLA Modules:
  0.0 219.2 jit_solution(14635899553552132513)
XLA Ops:
  7.2 0.0 copy-start
  7.2 0.0 copy-start.4
  7.2 0.0 copy-start.3
  7.2 0.0 copy-start.2
  7.2 0.0 all-reduce.2.cloned.1.call-start
  7.3 7.7 %convert_reduce_fusion = (f32[4096]{0:T(1024)S(1)}, f32[4096]{0:T(1024)S(1)}) fusion(bf16[2048,4096]{1,0:T(8,128)(2,1)} %param.5), kind=kLoop, calls=%fused_computation.2 | loop fusion | flops 33546240 | bytes 16809984 | tf_op jit(solution)/shard_map/reduce_sum | solution.py:374
  15.0 12.8 %shard_map.68 = f32[64,128]{1,0:T(8,128)S(1)} custom-call(f32[64,128]{1,0:T(8,128)S(1)} %pad_maximum_fusion.x_ref), custom_call_target="tpu_custom_call" | custom-call | tf_op jit(solution)/shard_map/pallas_call | solution.py:84
  27.8 0.0 copy-done.4
  27.8 0.0 copy-done.3
  27.8 0.2 fusion.10
  28.0 0.0 copy-done.2
  28.0 0.0 copy-done
  28.1 9.9 %fusion.5 = f32[2048,256]{1,0:T(8,128)} fusion(bf16[4096,256]{1,0:T(8,128)(2,1)S(1)} %copy-done, bf16[2048,4096]{1,0:T(8,128)(2,1)} %param.5, f32[4096]{0:T(1024)S(1)} %fusion.15, f32[4096]{0:T(1024)S(1)} %multiply_bitcast_fusion), kind=kOutput, calls=%fused_computation.7 | convolution fusion | flops 4328521728 | bytes 21004288 | tf_op jit(solution)/shard_map/dot_general | solution.py:383
  37.9 0.0 all-reduce.2.cloned.1.call-update
  38.0 20.7 %all-reduce.2.cloned.1.call-done.s_ref = f32[2048,256]{1,0:T(8,128)} async-done(((f32[2048,256]{1,0:T(8,128)}), f32[2048,256]{1,0:T(8,128)}) %all-reduce.2.cloned.1.call-update) | async-done | bytes 2097168 | tf_op jit(solution)/shard_map/psum | solution.py:384
  58.7 2.6 %subtract_convert_fusion = (bf16[2048,256]{1,0:T(8,128)(2,1)S(1)}, bf16[2048,256]{1,0:T(8,128)(2,1)S(1)}) fusion(f32[2048,256]{1,0:T(8,128)} %all-reduce.2.cloned.1.call-done.s_ref), kind=kLoop, calls=%fused_computation.12 | loop fusion | flops 2097152 | bytes 4194304 | tf_op jit(solution)/shard_map/convert_element_type | solution.py:386
  61.3 12.0 %fusion.3 = f32[512,4096]{1,0:T(8,128)S(1)} fusion(bf16[2048,4096]{1,0:T(8,128)(2,1)} %param.5, f32[4096]{0:T(1024)S(1)} %fusion.15, f32[4096]{0:T(1024)S(1)} %multiply_bitcast_fusion, bf16[2048,256]{1,0:T(8,128)(2,1)S(1)} %get-tuple-element.4, bf16[2048,256]{1,0:T(8,128)(2,1)S(1)} %get-tuple-element.5), kind=kOutput, calls=%fused_computation.6 | convolution fusion | flops 8627683328 | bytes 27295744 | tf_op jit(solution)/shard_map/dot_general | solution.py:388
  73.3 0.0 copy-start.1
  73.3 2.6 %slice_add_fusion.y_ref = f32[256,4096]{1,0:T(8,128)} fusion(f32[512,4096]{1,0:T(8,128)S(1)} %fusion.3), kind=kLoop, calls=%fused_computation.8 | loop fusion | flops 1048576 | bytes 12582912 | tf_op jit(solution)/shard_map/add | solution.py:390
  75.9 0.0 copy-done.1
  75.9 134.3 %shard_map.69 = (bf16[1024,256]{1,0:T(8,128)(2,1)S(1)}, bf16[256,4096]{1,0:T(8,128)(2,1)S(1)}) custom-call(f32[2048,256]{1,0:T(8,128)S(1)} %copy-done.1, f32[256,4096]{1,0:T(8,128)} %slice_add_fusion.y_ref), custom_call_target="tpu_custom_call" | custom-call | tf_op jit(solution)/shard_map/pallas_call | solution.py:344
  210.2 0.8 copy.10
  211.0 1.3 copy.11
  (3 shorter events, 0.0 us)
Async XLA Ops:
  7.2 20.9 %copy-start = (bf16[4096,256]{1,0:T(8,128)(2,1)S(1)}, bf16[4096,256]{1,0:T(8,128)(2,1)}, u32[]{:S(2)}) copy-start(bf16[4096,256]{1,0:T(8,128)(2,1)} %param.6) | copy-start | bytes 6291460
  7.2 20.6 %copy-start.4 = (f32[16]{0:T(128)S(1)}, f32[16]{0:T(128)}, u32[]{:S(2)}) copy-start(f32[16]{0:T(128)} %param.9) | copy-start | bytes 196
  7.2 20.6 %copy-start.3 = (s32[4096]{0:T(1024)S(1)}, s32[4096]{0:T(1024)}, u32[]{:S(2)}) copy-start(s32[4096]{0:T(1024)} %param.8) | copy-start | bytes 49156
  7.2 20.8 %copy-start.2 = (s32[4096]{0:T(1024)S(1)}, s32[4096]{0:T(1024)}, u32[]{:S(2)}) copy-start(s32[4096]{0:T(1024)} %param.7) | copy-start | bytes 49156
  7.2 51.5 %all-reduce.2.cloned.1.call-start = ((), (), s32[]{:S(2)}) async-start(), calls=%async_computation | async-start | bytes 4194304 | tf_op jit(solution)/shard_map/psum | solution.py:384
  73.3 2.6 %copy-start.1 = (f32[2048,256]{1,0:T(8,128)S(1)}, f32[2048,256]{1,0:T(8,128)}, u32[]{:S(2)}) copy-start(f32[2048,256]{1,0:T(8,128)} %all-reduce.2.cloned.1.call-done.s_ref) | copy-start | bytes 6291460
Sparse Core Ops, SparseCore 0:
  38.1 20.5 all-reduce.1

commit v2 on v1

--- a/solution.py
+++ b/solution.py
@@ -14,6 +14,8 @@
 LANES = 128
 BLOCK = 64
 QUARTERS = 4
+TILE = 256
+CHUNKS = 4
 
 
 def column_factor(col_mean, col_square, col_types, col_weight):
@@ -50,7 +52,7 @@
     pl.semaphore_wait(barrier, count)
 
 
-def group_sum(value, buf, send_sem, recv_sem, me, my_var, shift, size):
+def group_start(value, buf, send_sem, recv_sem, me, my_var, shift, size):
     place = group_place(me, shift, size)
     buf[place] = value
     copies = []
@@ -61,10 +63,14 @@
             device_id=(other, my_var), device_id_type=MESH)
         copy.start()
         copies.append(copy)
+    return copies
+
+
+def group_finish(buf, copies):
     for copy in copies:
         copy.wait()
     total = buf[0]
-    for i in range(1, size):
+    for i in range(1, len(copies) + 1):
         total = total + buf[i]
     return total
 
@@ -75,7 +81,8 @@
     greet(me, groups, my_var, 1)
     current = x_ref[...]
     for g, (shift, size) in enumerate(groups):
-        current = group_sum(current, buf.at[g], send_sem.at[g], recv_sem.at[g], me, my_var, shift, size)
+        sent = group_start(current, buf.at[g], send_sem.at[g], recv_sem.at[g], me, my_var, shift, size)
+        current = group_finish(buf.at[g], sent)
     o_ref[...] = current
 
 
@@ -136,9 +143,9 @@
     return orders, halvings
 
 
-def main_kernel(n_rec, n_var, total_rows, s_ref, y_ref, scores_ref, out_ref,
-                y_buf, got, full, gram, gram_rs, gram_ar, aug,
-                rs_send, rs_recv, ag_send, ag_recv, g_send, g_recv, y_sem):
+def main_kernel(n_rec, n_var, total_rows, part_ref, mean_ref, factor_ref, rec_ref, scores_ref, out_ref,
+                s_ref, s_got, s_pair, raw, tile, y_buf, got, full, gram, gram_rs, gram_ar, aug,
+                rs_send, rs_recv, ag_send, ag_recv, g_send, g_recv, s_send, s_recv, raw_sem):
     me, my_var = lax.axis_index("rec"), lax.axis_index("var")
     k_dim, columns = y_buf.shape
     groups = rec_groups(n_rec)
@@ -146,10 +153,25 @@
     n_stages = len(orders[0])
     part_cols = columns // 2
     part_rows = k_dim // QUARTERS
-    load = pltpu.make_async_copy(y_ref, y_buf, y_sem)
-    load.start()
-
+    n_tiles = columns // TILE
+    rows_dev = s_ref.shape[0]
+    chunk = rows_dev // CHUNKS
+
+    def raw_copy(i, slot):
+        return pltpu.make_async_copy(rec_ref.at[:, lanes_at(i * TILE, TILE)], raw.at[slot], raw_sem.at[slot])
+
+    raw_copy(0, 0).start()
     greet(me, groups, my_var, n_var)
+
+    def sketch_copy(c):
+        rows = pl.ds(c * chunk, chunk)
+        return pltpu.make_async_remote_copy(
+            src_ref=part_ref.at[rows, :], dst_ref=s_got.at[rows, :], send_sem=s_send.at[c], recv_sem=s_recv.at[c],
+            device_id=(me, 1 - my_var), device_id_type=MESH)
+
+    if n_var == 2:
+        for c in range(CHUNKS):
+            sketch_copy(c).start()
 
     def bit_of(j):
         return lax.rem(lax.div(me, 1 << j), 2)
@@ -199,8 +221,11 @@
                     rows = pl.ds(q * part_rows, part_rows)
                     lanes = lanes_at(base[s], held[s])
                     y_buf[rows, lanes] = y_buf[rows, lanes] + got[p, rows, pl.ds(got_at[s - 1], held[s])]
-                if s < n_stages:
+                if 0 < s < n_stages:
                     rs_copy(p, q, s).start()
+
+    def rs_begin(p, q):
+        rs_copy(p, q, 0).start()
 
     rs_left = list(range(QUARTERS + n_stages))
 
@@ -209,19 +234,46 @@
             if rs_left:
                 rs_step(rs_left.pop(0))
 
-    rows_dev = s_ref.shape[0]
-    step_rows = 256
-
-    def gram_step(i, total):
-        part = s_ref[rows_at(i * step_rows, step_rows), :]
-        return total + lax.dot_general(part, part, (((0,), (0,)), ((), ())), precision=highest,
-                                       preferred_element_type=jnp.float32)
-
-    gram[0] = lax.fori_loop(0, rows_dev // step_rows, gram_step, jnp.zeros((k_dim, k_dim), jnp.float32))
+    total = jnp.zeros((k_dim, k_dim), jnp.float32)
+    for c in range(CHUNKS):
+        rows = pl.ds(c * chunk, chunk)
+        part = part_ref[rows, :]
+        if n_var == 2:
+            sketch_copy(c).wait()
+            part = part + s_got[rows, :]
+        s_ref[rows, :] = part
+        turned = part.T
+        upper = turned.astype(jnp.bfloat16)
+        s_pair[:k_dim, rows] = upper
+        s_pair[k_dim:, rows] = (turned - upper.astype(jnp.float32)).astype(jnp.bfloat16)
+        total = total + jnp.dot(turned, part, precision=highest, preferred_element_type=jnp.float32)
+    gram[0] = total
+
+    def products(first, last):
+        def one(i, carry):
+            slot = lax.rem(i, 2)
+
+            @pl.when(i + 1 < n_tiles)
+            def _():
+                raw_copy(i + 1, 1 - slot).start()
+
+            raw_copy(i, slot).wait()
+            lanes = lanes_at(i * TILE, TILE)
+            mean, factor = mean_ref[:, lanes], factor_ref[:, lanes]
+            for c in range(CHUNKS):
+                rows = pl.ds(c * chunk, chunk)
+                tile[rows, :] = ((raw[slot, rows, :].astype(jnp.float32) - mean) * factor).astype(jnp.bfloat16)
+            pair = jnp.dot(s_pair[...], tile[...], preferred_element_type=jnp.float32)
+            y_buf[:, lanes] = pair[:k_dim] + pair[k_dim:]
+            return carry
+
+        lax.fori_loop(first, last, one, 0)
+
     half = k_dim // n_var
     shift, size = groups[0]
     piece = half // size
     place = group_place(me, shift, size)
+    cuts = [n_tiles * i // 4 for i in range(5)]
     copies = []
     for k in range(1, size):
         other_place = lax.rem(place + k, size)
@@ -234,14 +286,17 @@
         copies.append(copy)
     own_rows = rows_at(my_var * half + place * piece, piece)
     gram_rs[place] = gram[0, own_rows, :]
-    load.wait()
+    products(cuts[0], cuts[1])
     for copy in copies:
         copy.wait()
     current = gram_rs[0]
     for i in range(1, size):
         current = current + gram_rs[i]
     for g in range(1, len(groups)):
-        current = group_sum(current, gram_ar.at[g - 1], g_send.at[g], g_recv.at[g], me, my_var, *groups[g])
+        sent = group_start(current, gram_ar.at[g - 1], g_send.at[g], g_recv.at[g], me, my_var, *groups[g])
+        if g == 1:
+            products(cuts[1], cuts[2])
+        current = group_finish(gram_ar.at[g - 1], sent)
     gram[1, own_rows, :] = current
     copies = []
     last = len(groups)
@@ -253,6 +308,9 @@
             device_id=(me + (other_place - place) * shift, my_var), device_id_type=MESH)
         copy.start()
         copies.append(copy)
+    for q in range(QUARTERS):
+        rs_begin(0, q)
+    products(cuts[2], cuts[3])
     for copy in copies:
         copy.wait()
     copies = []
@@ -264,7 +322,10 @@
             device_id=(me, lax.rem(my_var + k, n_var)), device_id_type=MESH)
         copy.start()
         copies.append(copy)
-    advance()
+    products(cuts[3], cuts[4])
+    for q in range(QUARTERS):
+        rs_begin(1, q)
+    rs_left.pop(0)
     for copy in copies:
         copy.wait()
 
@@ -327,9 +388,9 @@
             scores_ref[t * n:(t + 1) * n, :] = (basis * math.sqrt(total_rows)).astype(scores_ref.dtype)
 
 
-def factor_and_project(sketch, products, n_rec, n_var, total_rows):
-    rows_dev, k_dim = sketch.shape
-    columns = products.shape[1]
+def factor_and_project(partial_sketch, col_mean, factor, records, n_rec, n_var, total_rows):
+    rows_dev, k_dim = partial_sketch.shape
+    columns = records.shape[1]
     groups = rec_groups(n_rec)
     orders, halvings = stage_plan(n_rec, columns)
     n_stages = len(orders[0])
@@ -347,9 +408,14 @@
             jax.ShapeDtypeStruct((rows_dev // n_var, k_dim), jnp.bfloat16),
             jax.ShapeDtypeStruct((k_dim, columns), jnp.bfloat16),
         ),
-        in_specs=[vmem, pl.BlockSpec(memory_space=pl.ANY)],
+        in_specs=[vmem, vmem, vmem, pl.BlockSpec(memory_space=pl.ANY)],
         out_specs=(vmem, vmem),
         scratch_shapes=[
+            pltpu.VMEM((rows_dev, k_dim), jnp.float32),
+            pltpu.VMEM((rows_dev, k_dim), jnp.float32),
+            pltpu.VMEM((2 * k_dim, rows_dev), jnp.bfloat16),
+            pltpu.VMEM((2, rows_dev, TILE), jnp.bfloat16),
+            pltpu.VMEM((rows_dev, TILE), jnp.bfloat16),
             pltpu.VMEM((k_dim, columns), jnp.float32),
             pltpu.VMEM((2, k_dim, got_width), jnp.float32),
             pltpu.VMEM((k_dim, columns), jnp.float32),
@@ -360,10 +426,10 @@
             dma((2, QUARTERS, n_stages)), dma((2, QUARTERS, n_stages)),
             dma((2, QUARTERS, n_stages)), dma((2, QUARTERS, n_stages)),
             dma((len(groups) + 2, max(4, n_var))), dma((len(groups) + 2, max(4, n_var))),
-            dma,
+            dma((CHUNKS,)), dma((CHUNKS,)), dma((2,)),
         ],
         compiler_params=pltpu.CompilerParams(collective_id=1, has_side_effects=True, vmem_limit_bytes=48 << 20),
-    )(sketch, products)
+    )(partial_sketch, col_mean[None, :], factor[None, :], records)
 
 
 def local(records, test_matrix, col_types, col_groups, group_weight):
@@ -381,14 +447,9 @@
     factor = column_factor(col_mean, sums[1] / total_rows, col_types, col_weight)
     scaled = ((values - col_mean) * factor).astype(jnp.bfloat16)
     partial_sketch = jnp.dot(scaled, test_matrix, preferred_element_type=jnp.float32)
-    sketch = lax.psum(partial_sketch, "var")
-    upper = sketch.astype(jnp.bfloat16)
-    lower = (sketch - upper.astype(jnp.float32)).astype(jnp.bfloat16)
-    both = jnp.concatenate([upper, lower], axis=1)
-    pair = lax.dot_general(both, scaled, (((0,), (0,)), ((), ())), preferred_element_type=jnp.float32)
-    k_dim = test_matrix.shape[1]
-    products = pair[:k_dim] + pair[k_dim:]
-    return factor_and_project(sketch, products, n_rec, n_var, total_rows)
+    if n_var != 2:
+        partial_sketch = lax.psum(partial_sketch, "var")
+    return factor_and_project(partial_sketch, col_mean, factor, records, n_rec, n_var, total_rows)
 
 
 def solution(mesh):

time: 219 us -> 173 us (0.79)
  waiting for transfers between devices: 20.8 us -> 0 us
  between operations: 14.2 us -> 0.72 us
  matrix products: 22.1 us -> 9.21 us
  Pallas kernels: 147 us -> 153 us
  other arithmetic: 12.9 us -> 7.53 us
    psum x1 -> x0, waiting for transfers between devices: 20.7 us -> none  [local(): sketch = lax.psum(partial_sketch, 'var')]
    dot_general x1 -> x0, matrix products: 12 us -> none  [local(): lax.dot_general(both, scaled, (((0,), (0,)), ((), ())), preferred_element...]
    pallas_call x1, Pallas kernels: 134 us -> 140 us  [factor_and_project(): pl.pallas_call(functools.partial(main_kernel, n_rec, n_var, total_rows),...]
    convert_element_type x1 -> x0, other arithmetic: 2.6 us -> none  [local(): lower = (sketch - upper.astype(jnp.float32)).astype(jnp.bfloat16)]
    add x1 -> x0, other arithmetic: 2.59 us -> none  [local(): products = pair[:k_dim] + pair[k_dim:]]
  transfers between devices with their start and end apart: 1 -> 0, of which waited for: 1 -> 0; matrix products, arithmetic and copies ran while one was open for 0% -> 0% of each run, Pallas kernels for 0% -> 0%
where the time goes in v2:
time: 173 us
  Pallas kernels  153 us (88%)
  matrix products  9.21 us (5%)
  other arithmetic  7.53 us (4%)
  local copies, waits for them, and re-layouts  2.13 us (1%)
    pallas_call x1, Pallas kernels, factor_and_project(): pl.pallas_call(functools.partial(main_kernel, n_rec, n_var, total_rows),...  140 us
    pallas_call x1, Pallas kernels, sum_over_rec(): pl.pallas_call(functools.partial(stats_kernel, n_rec), out_shape=jax.Shap...  12.8 us
    dot_general x1, matrix products, local(): jnp.dot(scaled, test_matrix, preferred_element_type=jnp.float32)  8.14 us
    reduce_sum x1, other arithmetic, local(): jnp.sum(values, 0)  7.51 us

profile of v2, /device:TPU:0, one launch (start us, length us, event | category | flops | bytes accessed | tf_op | source)
XLA Modules:
  0.0 172.8 jit_solution(8712771537644893928)
XLA Ops:
  0.6 0.0 copy-start
  0.6 0.0 copy-start.1
  0.7 1.1 fusion.7
  1.7 7.5 %convert_reduce_fusion = (f32[4096]{0:T(1024)S(1)}, f32[4096]{0:T(1024)S(1)}) fusion(bf16[2048,4096]{1,0:T(8,128)(2,1)} %rec_ref.1), kind=kLoop, calls=%fused_computation.2 | loop fusion | flops 33546240 | bytes 16809984 | tf_op jit(solution)/shard_map/reduce_sum | solution.py:440
  9.3 12.8 %shard_map.68 = f32[64,128]{1,0:T(8,128)S(1)} custom-call(f32[64,128]{1,0:T(8,128)S(1)} %pad_maximum_fusion.x_ref), custom_call_target="tpu_custom_call" | custom-call | tf_op jit(solution)/shard_map/pallas_call | solution.py:91
  22.0 0.0 copy-done.1
  22.1 0.0 copy-done
  22.1 8.1 %fusion.3.part_ref = f32[2048,256]{1,0:T(8,128)S(1)} fusion(bf16[4096,256]{1,0:T(8,128)(2,1)S(1)} %copy-done, bf16[2048,4096]{1,0:T(8,128)(2,1)} %rec_ref.1, f32[4096]{0:T(1024)S(1)} %fusion.12, f32[4096]{0:T(1024)S(1)} %get-tuple-element.5), kind=kOutput, calls=%fused_computation.6 | convolution fusion | flops 4328521728 | bytes 21004288 | tf_op jit(solution)/shard_map/dot_general | solution.py:449
  30.2 140.4 %shard_map.69 = (bf16[1024,256]{1,0:T(8,128)(2,1)S(1)}, bf16[256,4096]{1,0:T(8,128)(2,1)S(1)}) custom-call(f32[2048,256]{1,0:T(8,128)S(1)} %fusion.3.part_ref, f32[1,4096]{1,0:T(1,128)S(1)} %bitcast.23, f32[1,4096]{1,0:T(1,128)S(1)} %bitcast.22, bf16[2048,4096]{1,0:T(8,128)(2,1)} %rec_ref.1), custom_call_target="tpu_custom_call" | custom-call | tf_op jit(solution)/shard_map/pallas_call | solution.py:405
  170.6 0.8 copy.9
  171.4 1.3 copy.10
  (3 shorter events, 0.0 us)
Async XLA Ops:
  0.6 21.4 %copy-start = (bf16[4096,256]{1,0:T(8,128)(2,1)S(1)}, bf16[4096,256]{1,0:T(8,128)(2,1)}, u32[]{:S(2)}) copy-start(bf16[4096,256]{1,0:T(8,128)(2,1)} %param.6) | copy-start | bytes 6291460
  0.6 21.4 %copy-start.1 = (s32[4096]{0:T(1024)S(1)}, s32[4096]{0:T(1024)}, u32[]{:S(2)}) copy-start(s32[4096]{0:T(1024)} %param.7) | copy-start | bytes 49156

commit v3 on v2

--- a/solution.py
+++ b/solution.py
@@ -110,7 +110,7 @@
     return pl.ds(pl.multiple_of(start, LANES), size)
 
 
-def factor_block(block):
+def factor_block(block, between):
     tiles_n = BLOCK // 8
     lane = lax.broadcasted_iota(jnp.int32, (8, LANES), 1)
     row = lax.broadcasted_iota(jnp.int32, (8, LANES), 0)
@@ -119,6 +119,8 @@
         eye = (lane == row + (BLOCK + 8 * t)).astype(jnp.float32)
         tiles.append(jnp.where(lane < BLOCK, block[8 * t:8 * t + 8, :], eye))
     for j in range(BLOCK - 1):
+        if j in (BLOCK // 4, BLOCK // 2, 3 * BLOCK // 4):
+            between()
         own, sub = j // 8, j % 8
         pivot_row = tiles[own][sub:sub + 1, :]
         scaled_row = pivot_row / pivot_row[:, j:j + 1]
@@ -157,8 +159,17 @@
     rows_dev = s_ref.shape[0]
     chunk = rows_dev // CHUNKS
 
+    def tile_at(i):
+        quarter = n_tiles // 4
+        turn = lax.div(jnp.int32(i), quarter)
+        part, stays = lax.rem(turn, 2), lax.div(turn, 2)
+        bits = [lax.rem(lax.div(me, 1 << orders[p][0]), 2) for p in range(2)]
+        bit = bits[0] + part * (bits[1] - bits[0])
+        which = stays * bit + (1 - stays) * (1 - bit)
+        return (part * 2 + which) * quarter + lax.rem(jnp.int32(i), quarter)
+
     def raw_copy(i, slot):
-        return pltpu.make_async_copy(rec_ref.at[:, lanes_at(i * TILE, TILE)], raw.at[slot], raw_sem.at[slot])
+        return pltpu.make_async_copy(rec_ref.at[:, lanes_at(tile_at(i) * TILE, TILE)], raw.at[slot], raw_sem.at[slot])
 
     raw_copy(0, 0).start()
     greet(me, groups, my_var, n_var)
@@ -227,12 +238,16 @@
     def rs_begin(p, q):
         rs_copy(p, q, 0).start()
 
-    rs_left = list(range(QUARTERS + n_stages))
-
-    def advance(n=1):
-        for _ in range(n):
-            if rs_left:
-                rs_step(rs_left.pop(0))
+    n_steps = QUARTERS + n_stages - 1
+    rs_left = list(range(1, n_steps + 1))
+
+    n_calls = 5 * (k_dim // BLOCK) - 1
+    calls = []
+
+    def advance():
+        calls.append(len(calls))
+        while rs_left and (n_steps - len(rs_left)) * n_calls < len(calls) * n_steps:
+            rs_step(rs_left.pop(0))
 
     total = jnp.zeros((k_dim, k_dim), jnp.float32)
     for c in range(CHUNKS):
@@ -258,7 +273,7 @@
                 raw_copy(i + 1, 1 - slot).start()
 
             raw_copy(i, slot).wait()
-            lanes = lanes_at(i * TILE, TILE)
+            lanes = lanes_at(tile_at(i) * TILE, TILE)
             mean, factor = mean_ref[:, lanes], factor_ref[:, lanes]
             for c in range(CHUNKS):
                 rows = pl.ds(c * chunk, chunk)
@@ -309,7 +324,8 @@
         copy.start()
         copies.append(copy)
     for q in range(QUARTERS):
-        rs_begin(0, q)
+        for p in range(2):
+            rs_begin(p, q)
     products(cuts[2], cuts[3])
     for copy in copies:
         copy.wait()
@@ -323,9 +339,6 @@
         copy.start()
         copies.append(copy)
     products(cuts[3], cuts[4])
-    for q in range(QUARTERS):
-        rs_begin(1, q)
-    rs_left.pop(0)
     for copy in copies:
         copy.wait()
 
@@ -340,7 +353,7 @@
         block = aug[rows, lane_at:lane_at + LANES]
         if b * BLOCK != lane_at:
             block = pltpu.roll(block, LANES - BLOCK, axis=1)
-        inverse = factor_block(block)
+        inverse = factor_block(block, advance)
         advance()
         solved = jnp.dot(inverse, aug[rows, :], precision=highest, preferred_element_type=jnp.float32)
         aug[rows, :] = solved
@@ -350,7 +363,8 @@
             rest = slice((b + 1) * BLOCK, k_dim)
             aug[rest, :] = aug[rest, :] - change[rest, :]
             advance()
-    advance(len(rs_left))
+    for t in rs_left:
+        rs_step(t)
 
     for p in range(2):
         base, held = bases[p]

time: 173 us -> 167 us (0.965)
  Pallas kernels: 153 us -> 147 us
    pallas_call x1, Pallas kernels: 140 us -> 135 us  [factor_and_project(): pl.pallas_call(functools.partial(main_kernel, n_rec, n_var, total_rows),...]
where the time goes in v3:
time: 167 us
  Pallas kernels  147 us (88%)
  matrix products  9.21 us (6%)
  other arithmetic  7.53 us (5%)
  local copies, waits for them, and re-layouts  2.13 us (1%)
    pallas_call x1, Pallas kernels, factor_and_project(): pl.pallas_call(functools.partial(main_kernel, n_rec, n_var, total_rows),...  135 us
    pallas_call x1, Pallas kernels, sum_over_rec(): pl.pallas_call(functools.partial(stats_kernel, n_rec), out_shape=jax.Shap...  12.8 us
    dot_general x1, matrix products, local(): jnp.dot(scaled, test_matrix, preferred_element_type=jnp.float32)  8.14 us
    reduce_sum x1, other arithmetic, local(): jnp.sum(values, 0)  7.51 us

profile of v3, /device:TPU:0, one launch (start us, length us, event | category | flops | bytes accessed | tf_op | source)
XLA Modules:
  0.0 166.9 jit_solution(12404895831068277842)
XLA Ops:
  0.6 0.0 copy-start
  0.6 0.0 copy-start.1
  0.7 1.1 fusion.7
  1.7 7.5 %convert_reduce_fusion = (f32[4096]{0:T(1024)S(1)}, f32[4096]{0:T(1024)S(1)}) fusion(bf16[2048,4096]{1,0:T(8,128)(2,1)} %rec_ref.1), kind=kLoop, calls=%fused_computation.2 | loop fusion | flops 33546240 | bytes 16809984 | tf_op jit(solution)/shard_map/reduce_sum | solution.py:454
  9.3 12.8 %shard_map.68 = f32[64,128]{1,0:T(8,128)S(1)} custom-call(f32[64,128]{1,0:T(8,128)S(1)} %pad_maximum_fusion.x_ref), custom_call_target="tpu_custom_call" | custom-call | tf_op jit(solution)/shard_map/pallas_call | solution.py:91
  22.0 0.0 copy-done.1
  22.1 0.0 copy-done
  22.1 8.1 %fusion.3.part_ref = f32[2048,256]{1,0:T(8,128)S(1)} fusion(bf16[4096,256]{1,0:T(8,128)(2,1)S(1)} %copy-done, bf16[2048,4096]{1,0:T(8,128)(2,1)} %rec_ref.1, f32[4096]{0:T(1024)S(1)} %fusion.12, f32[4096]{0:T(1024)S(1)} %get-tuple-element.5), kind=kOutput, calls=%fused_computation.6 | convolution fusion | flops 4328521728 | bytes 21004288 | tf_op jit(solution)/shard_map/dot_general | solution.py:463
  30.2 134.6 %shard_map.69 = (bf16[1024,256]{1,0:T(8,128)(2,1)S(1)}, bf16[256,4096]{1,0:T(8,128)(2,1)S(1)}) custom-call(f32[2048,256]{1,0:T(8,128)S(1)} %fusion.3.part_ref, f32[1,4096]{1,0:T(1,128)S(1)} %bitcast.23, f32[1,4096]{1,0:T(1,128)S(1)} %bitcast.22, bf16[2048,4096]{1,0:T(8,128)(2,1)} %rec_ref.1), custom_call_target="tpu_custom_call" | custom-call | tf_op jit(solution)/shard_map/pallas_call | solution.py:419
  164.8 0.8 copy.9
  165.6 1.3 copy.10
  (3 shorter events, 0.0 us)
Async XLA Ops:
  0.6 21.4 %copy-start = (bf16[4096,256]{1,0:T(8,128)(2,1)S(1)}, bf16[4096,256]{1,0:T(8,128)(2,1)}, u32[]{:S(2)}) copy-start(bf16[4096,256]{1,0:T(8,128)(2,1)} %param.6) | copy-start | bytes 6291460
  0.6 21.4 %copy-start.1 = (s32[4096]{0:T(1024)S(1)}, s32[4096]{0:T(1024)}, u32[]{:S(2)}) copy-start(s32[4096]{0:T(1024)} %param.7) | copy-start | bytes 49156
